TPU v7x, 256 devices: a whole 4x4x8 slice. The times are simulated.
256 devices in a mesh: elem: 64 (over y_lo, z, x), mode: 4 (over y_hi, core).
Axes of the slice: x: 4, y: 4 (y_hi: 2, y_lo: 2; y = y_hi * 2 + y_lo), z: 8, core: 2. Of those that a mesh axis runs over, the one named last changes fastest.
Arguments:
- velocity: float32 [3, 512, 65536], P(None, 'mode', 'elem'), may hold values from -6 to 6
- metric: float32 [4, 65536], P(None, 'elem'), may hold values from 0.5 to 2
- lift: float32 [1024, 32, 64], P('elem'), may hold values from -1.5 to 1.5
- blocks: float32 [1024, 32, 32], P('elem'), may hold values from -2.1 to 4, as said below
- conn: int32 [1024, 4], P('elem'), may hold values from 0 to 39, as said below
- send_list: int32 [64, 8], P('elem'), may hold values from 0 to 31, as said below
Outputs:
- velocity_new: float32 [3, 512, 65536], P(None, 'mode', 'elem')
- trace: float32 [2048, 8, 3, 512], P('elem', None, None, 'mode')
Inputs may be any that keep to these rules, and one draw needn't show every extreme that they name: `blocks`: diagonal entries lie in 2 to 4, off-diagonal ones within -2.1 to 2.1. `conn`: rows d * 16 to (d + 1) * 16 - 1 belong to partition d. A slot below 32 is one of partition d's faces; slot 32 + k stands for face send_list[d - 1, k] of partition d - 1. Every slot of 32 to 39 is used by exactly one element of the partition, every face of the partition by one or two of its elements. `send_list`: row d holds 8 distinct faces of partition d, each used by exactly one of partition d's elements.
All inputs are finite; a program needn't handle non-finite values.
Results may differ from a plain program's by a relative error of at most 0.0001.
Values sent between devices are 32-bit elements; how exact they have to be, the bound alone decides.
No kernel may reach another device: no remote copies, remote signals or barrier semaphores. Data moves between devices by JAX's collectives and lax.ppermute only.
A program may use at most 64 MiB of HBM per device.

v0:
```python
import math

import jax
import jax.numpy as jnp
from jax import lax
from jax.sharding import PartitionSpec as P

NODES1 = 8
SWEEPS = 8


HIGHEST = lax.Precision.HIGHEST
TIME_STEP = 0.01
RELAXATION = 0.8
HELMHOLTZ_BASE = 0.5


def from_behind(array, axis, by):
    size = lax.axis_size(axis)
    pairs = [(i, i + by) for i in range(size) if 0 <= i + by < size]
    return lax.ppermute(array, axis, pairs)


def edge_derivative(length):
    index = jnp.arange(length, dtype=jnp.int32)
    points_at = jnp.cos(math.pi * index.astype(jnp.float32) / (length - 1))
    weights = jnp.where((index == 0) | (index == length - 1), 2.0, 1.0).astype(jnp.float32)
    parity = ((index[:, None] + index[None, :]) % 2).astype(jnp.float32)
    signs = 1.0 - 2.0 * parity
    diagonal_mask = index[:, None] == index[None, :]
    spacing = jnp.where(diagonal_mask, 1.0, points_at[:, None] - points_at[None, :])
    offdiag = jnp.where(diagonal_mask, 0.0, weights[:, None] / weights[None, :] * signs / spacing)
    return offdiag - jnp.diag(jnp.sum(offdiag, axis=1))


def node_tables(length):
    edge = edge_derivative(length)
    eye_edge = jnp.eye(length, dtype=jnp.float32)
    return (jnp.kron(eye_edge, edge), jnp.kron(edge, eye_edge))


def plane_tables(length):
    plane = jnp.arange(length, dtype=jnp.int32)[:, None]
    column = jnp.arange(length, dtype=jnp.int32)[None, :]
    wave = (column + 1) // 2
    phase = wave * plane % length
    angle = 2.0 * math.pi / length * phase.astype(jnp.float32)
    is_sine = (column % 2 == 0) & (column > 0)
    is_edge = (column == 0) | (column == length - 1)
    factor = jnp.where(is_edge, math.sqrt(1.0 / length), math.sqrt(2.0 / length)).astype(
        jnp.float32
    )
    rate = wave.astype(jnp.float32) * (8.0 / length)
    basis = factor * jnp.where(is_sine, jnp.sin(angle), jnp.cos(angle))
    slope = factor * rate * jnp.where(is_sine, jnp.cos(angle), -jnp.sin(angle))
    slope = jnp.where(column == length - 1, 0.0, slope)
    return (basis, slope, rate[0])


def shards(velocity, metric, lift, blocks, conn, send_list):
    mode_count = velocity.shape[1]
    planes = mode_count * lax.axis_size("mode")
    points = velocity.shape[2]
    point_share = points // lax.axis_size("mode")
    elem_count = lift.shape[0]
    block_width = lift.shape[1]
    node_count = lift.shape[2]
    face_nodes = block_width // 4
    face_count = 2 * elem_count
    halo_rows = send_list.shape[1]
    slot_count = face_count + halo_rows
    basis, slope, rate = plane_tables(planes)
    along_r, along_s = node_tables(NODES1)
    eye_pair = jnp.eye(2, dtype=jnp.float32)
    pair_r = jnp.kron(eye_pair, along_r)
    pair_s = jnp.kron(eye_pair, along_s)
    local_rate = lax.dynamic_slice_in_dim(rate, lax.axis_index("mode") * mode_count, mode_count)
    kappa = HELMHOLTZ_BASE + local_rate * local_rate
    local_metric = lax.dynamic_slice_in_dim(
        metric, lax.axis_index("mode") * point_share, point_share, 1
    )
    coeffs = lax.all_to_all(velocity, "mode", split_axis=2, concat_axis=1, tiled=True)
    items = coeffs.shape[0]
    physical = jnp.einsum("pm,cmq->cpq", basis, coeffs, precision=HIGHEST)
    along_z = jnp.einsum("pm,cmq->cpq", slope, coeffs, precision=HIGHEST)
    paired = physical.reshape(items, planes, point_share // (2 * node_count), 2 * node_count)
    by_r = jnp.einsum("kn,cpen->cpek", pair_r, paired, precision=HIGHEST).reshape(physical.shape)
    by_s = jnp.einsum("kn,cpen->cpek", pair_s, paired, precision=HIGHEST).reshape(physical.shape)
    grad_x = local_metric[0] * by_r + local_metric[1] * by_s
    grad_y = local_metric[2] * by_r + local_metric[3] * by_s
    physical, grad_x, grad_y, along_z = (physical, grad_x, grad_y, along_z)
    nonlinear = physical[0] * grad_x + physical[1] * grad_y + physical[2] * along_z
    spectral = jnp.einsum("pm,cpq->cmq", basis, nonlinear, precision=HIGHEST)
    advected = lax.all_to_all(spectral, "mode", split_axis=1, concat_axis=2, tiled=True)
    grouped = (velocity - TIME_STEP * advected).reshape(3, mode_count, elem_count, node_count)
    forcing_elem = jnp.einsum("ein,cmen->eicm", lift, grouped, precision=HIGHEST)
    face_slots = conn.reshape(-1)
    assembly = (face_slots[:, None] == jnp.arange(slot_count, dtype=jnp.int32)[None, :]).astype(
        jnp.float32
    )
    send_faces = send_list[0]
    picker = (send_faces[:, None] == jnp.arange(face_count, dtype=jnp.int32)[None, :]).astype(
        jnp.float32
    )

    def assemble(per_elem):
        rows = per_elem.reshape(elem_count * 4, face_nodes, 3, mode_count)
        return jnp.einsum("rs,rabc->sabc", assembly, rows, precision=HIGHEST)

    forcing_all = assemble(forcing_elem)
    diag_rows = jnp.diagonal(blocks, axis1=1, axis2=2).reshape(elem_count * 4, face_nodes)
    diag_all = jnp.einsum("rs,ra->sa", assembly, diag_rows, precision=HIGHEST)
    hits_all = jnp.sum(assembly, axis=0)
    back_forcing, back_diag, back_count = from_behind(
        (forcing_all[face_count:], diag_all[face_count:], hits_all[face_count:]), "elem", -1
    )
    forcing = forcing_all[:face_count] + jnp.einsum(
        "kf,kabc->fabc", picker, back_forcing, precision=HIGHEST
    )
    diag_sum = diag_all[:face_count] + jnp.einsum("kf,ka->fa", picker, back_diag, precision=HIGHEST)
    face_hits = hits_all[:face_count] + jnp.einsum("kf,k->f", picker, back_count, precision=HIGHEST)
    diag_scale = diag_sum[:, :, None, None] + kappa * face_hits[:, None, None, None]
    trace = RELAXATION * forcing / diag_scale
    values = None
    for sweep_index in range(1, SWEEPS + 1):
        outgoing = jnp.take(trace, send_faces, axis=0)
        incoming = from_behind(outgoing, "elem", 1)
        extended = jnp.concatenate([trace, incoming], axis=0)
        values = jnp.take(extended, face_slots, axis=0).reshape(
            elem_count, block_width, 3, mode_count
        )
        if sweep_index == SWEEPS:
            break
        products = jnp.einsum("eij,ejcm->eicm", blocks, values, precision=HIGHEST) + kappa * values
        summed = assemble(products)
        returned = from_behind(summed[face_count:], "elem", -1)
        applied = summed[:face_count] + jnp.einsum(
            "kf,kabc->fabc", picker, returned, precision=HIGHEST
        )
        trace = trace + RELAXATION * (forcing - applied) / diag_scale
    velocity_new = grouped + jnp.einsum("ein,eicm->cmen", lift, values, precision=HIGHEST)
    return (velocity_new.reshape(3, mode_count, points), trace)


def solution(mesh):
    return jax.shard_map(
        shards,
        mesh=mesh,
        in_specs=(
            P(None, "mode", "elem"),
            P(None, "elem"),
            P("elem", None, None),
            P("elem", None, None),
            P("elem", None),
            P("elem", None),
        ),
        out_specs=(P(None, "mode", "elem"), P("elem", None, None, "mode")),
        check_vma=False,
    )
```

profile of v0, /device:TPU:8, one launch (start us, length us, event | category | flops | bytes accessed | tf_op | source)
XLA Modules:
  0.0 316.4 jit_solution(3336930908105217957)
XLA Ops:
  0.6 2.9 copy.91
  3.5 3.7 %all-to-all-start = ((f32[3,128,1024]{1,0,2:T(4,128)}), f32[3,128,1024]{1,0,2:T(4,128)S(1)}, u32[]{:S(2)}, u32[]{:S(2)}) async-start(f32[3,128,1024]{1,0,2:T(4,128)} %copy.91), calls=%async_computation | async-start | bytes 4194304 | tf_op jit(solution)/shard_map/all_to_all | solution.py:82
  7.7 10.7 %collective-permute-start.2 = (f32[8]{0:T(128)S(1)}, f32[8]{0:T(128)S(1)}, u32[]{:S(2)}, u32[]{:S(2)}) collective-permute-start(f32[8]{0:T(128)S(1)} %slice.93), channel_id=1, source_target_pairs={{4,0},{8,4},{12,8},{16,12},{20,16},{24,20},{28,24},{32,28},{36,32}... | collective-permute-start | bytes 104 | tf_op jit(solution)/shard_map/ppermute | solution.py:21
  19.7 2.8 collective-permute-start.1
  22.6 3.0 copy.106
  27.7 6.8 %all-to-all-done = f32[3,128,1024]{1,0,2:T(4,128)S(1)} async-done(((f32[3,128,1024]{1,0,2:T(4,128)}), f32[3,128,1024]{1,0,2:T(4,128)S(1)}, u32[]{:S(2)}, u32[]{:S(2)}) %all-to-all-start) | async-done | bytes 1572896 | tf_op jit(solution)/shard_map/all_to_all | solution.py:82
  34.4 2.2 copy.234
  36.6 3.0 all_to_all.23
  39.6 8.2 %fusion.59 = f32[512,3,256]{0,2,1:T(8,128)S(1)} fusion(f32[3,512,256]{1,2,0:T(8,128)} %all_to_all.23, s32[512]{0:T(512)S(1)} %add_select_fusion.2, f32[512]{0:T(512)S(1)} %get-tuple-element.24, pred[512]{0:T(512)(128)(4,1)S(1)} %get-tuple-element.28), kind=kOutput, calls=%fused_computation.98 | convolution fusion | flops 2420113408 | bytes 3150336 | tf_op jit(solution)/shard_map/pm,cmq->cpq/dot_general | solution.py:84
  47.9 2.7 fusion.122
  50.6 3.0 copy.95
  53.6 2.8 fusion.120
  56.3 3.0 copy.97
  60.3 2.2 copy.101
  63.7 7.2 %fusion.56 = f32[512,3,256]{2,0,1:T(8,128)S(1)} fusion(f32[3,512,256]{1,2,0:T(8,128)S(1)} %copy-done.4, f32[512]{0:T(512)S(1)} %get-tuple-element.23, s32[512]{0:T(512)S(1)} %add_select_fusion.2, pred[512]{0:T(512)(128)(4,1)S(1)} %get-tuple-element.27, pred[512]{0:T(512)(128)(4,1)S(1)} %get-tuple-element.28), kind=kOutput, calls=%fused_computation.95 | convolution fusion | flops 2420637696 | bytes 3150848 | tf_op jit(solution)/shard_map/pm,cmq->cpq/dot_general | solution.py:85
  71.0 7.9 %fusion.11 = f32[3,512,256]{1,2,0:T(8,128)S(1)} fusion(f32[512,3,256]{2,0,1:T(8,128)S(1)} %fusion.56, f32[3,512,256]{2,1,0:T(8,128)S(1)} %copy-done.3, f32[3,512,256]{2,1,0:T(8,128)S(1)} %copy-done.2, f32[512,256]{1,0:T(8,128)S(1)} %copy-done.6, f32[256]{0:T(256)S(1)} %bitcast.222, f32[256]{0:T(256)S(1)} %bitcast.220, f32[512,256]{1,0:T(8,128)S(1)} %copy.98, ...), kind=kOutput, calls=%fused_computation.35 | convolution fusion | flops 2424438784 | bytes 7873024 | tf_op jit(solution)/shard_map/pm,cpq->cmq/dot_general | solution.py:93
  80.7 4.4 %all-to-all-start.1 = ((f32[3,512,256]{2,0,1:T(4,128)}), f32[3,512,256]{2,0,1:T(4,128)}, u32[]{:S(2)}, u32[]{:S(2)}) async-start(f32[3,512,256]{2,0,1:T(4,128)} %copy.104), calls=%async_computation.1 | async-start | bytes 4194304 | tf_op jit(solution)/shard_map/all_to_all | solution.py:94
  85.6 26.7 %all-to-all-done.1 = f32[3,512,256]{2,0,1:T(4,128)} async-done(((f32[3,512,256]{2,0,1:T(4,128)}), f32[3,512,256]{2,0,1:T(4,128)}, u32[]{:S(2)}, u32[]{:S(2)}) %all-to-all-start.1) | async-done | bytes 1572896 | tf_op jit(solution)/shard_map/all_to_all | solution.py:94
  112.4 2.1 broadcast_multiply_fusion
  116.1 2.0 bitcast_subtract_fusion
  119.9 10.7 %collective-permute-start = (f32[8,8,3,128]{3,0,2,1:T(8,128)S(1)}, f32[8,8,3,128]{3,0,2,1:T(8,128)S(1)}, u32[]{:S(2)}, u32[]{:S(2)}) collective-permute-start(f32[8,8,3,128]{3,0,2,1:T(8,128)S(1)} %slice.146), channel_id=1, source_target_pairs={{4,0},{8,4},{12,8},{16,12},{20,16},{24,20},{28,24},{32,28},{36,32}... | collective-permute-start | bytes 294920 | tf_op jit(solution)/shard_map/ppermute | solution.py:21
  130.7 2.1 collective-permute-done
  136.1 9.2 %collective-permute-done.3 = f32[8,8,3,128]{3,0,2,1:T(8,128)S(1)} collective-permute-done((f32[8,8,3,128]{3,0,2,1:T(8,128)S(1)}, f32[8,8,3,128]{3,0,2,1:T(8,128)S(1)}, u32[]{:S(2)}, u32[]{:S(2)}) %collective-permute-start.3) | collective-permute-done | bytes 98336 | tf_op jit(solution)/shard_map/ppermute | solution.py:21
  149.7 3.9 %collective-permute-start.4 = (f32[8,8,3,128]{3,0,2,1:T(8,128)S(1)}, f32[8,8,3,128]{3,0,2,1:T(8,128)S(1)}, u32[]{:S(2)}, u32[]{:S(2)}) collective-permute-start(f32[8,8,3,128]{3,0,2,1:T(8,128)S(1)} %slice.148), channel_id=1, source_target_pairs={{4,0},{8,4},{12,8},{16,12},{20,16},{24,20},{28,24},{32,28},{36,32}... | collective-permute-start | bytes 294920 | tf_op jit(solution)/shard_map/ppermute | solution.py:21
  153.6 2.6 collective-permute-done.4
  157.7 1.9 collective-permute-start.5
  159.6 8.8 %collective-permute-done.5 = f32[8,8,3,128]{3,0,2,1:T(8,128)S(1)} collective-permute-done((f32[8,8,3,128]{3,0,2,1:T(8,128)S(1)}, f32[8,8,3,128]{3,0,2,1:T(8,128)S(1)}, u32[]{:S(2)}, u32[]{:S(2)}) %collective-permute-start.5) | collective-permute-done | bytes 98336 | tf_op jit(solution)/shard_map/ppermute | solution.py:21
  173.0 3.9 %collective-permute-start.6 = (f32[8,8,3,128]{3,0,2,1:T(8,128)S(1)}, f32[8,8,3,128]{3,0,2,1:T(8,128)S(1)}, u32[]{:S(2)}, u32[]{:S(2)}) collective-permute-start(f32[8,8,3,128]{3,0,2,1:T(8,128)S(1)} %slice.150), channel_id=1, source_target_pairs={{4,0},{8,4},{12,8},{16,12},{20,16},{24,20},{28,24},{32,28},{36,32}... | collective-permute-start | bytes 294920 | tf_op jit(solution)/shard_map/ppermute | solution.py:21
  176.9 2.6 collective-permute-done.6
  181.0 2.1 collective-permute-start.7
  183.1 8.6 %collective-permute-done.7 = f32[8,8,3,128]{3,0,2,1:T(8,128)S(1)} collective-permute-done((f32[8,8,3,128]{3,0,2,1:T(8,128)S(1)}, f32[8,8,3,128]{3,0,2,1:T(8,128)S(1)}, u32[]{:S(2)}, u32[]{:S(2)}) %collective-permute-start.7) | collective-permute-done | bytes 98336 | tf_op jit(solution)/shard_map/ppermute | solution.py:21
  196.2 3.9 %collective-permute-start.8 = (f32[8,8,3,128]{3,0,2,1:T(8,128)S(1)}, f32[8,8,3,128]{3,0,2,1:T(8,128)S(1)}, u32[]{:S(2)}, u32[]{:S(2)}) collective-permute-start(f32[8,8,3,128]{3,0,2,1:T(8,128)S(1)} %slice.152), channel_id=1, source_target_pairs={{4,0},{8,4},{12,8},{16,12},{20,16},{24,20},{28,24},{32,28},{36,32}... | collective-permute-start | bytes 294920 | tf_op jit(solution)/shard_map/ppermute | solution.py:21
  200.2 2.6 collective-permute-done.8
  206.2 8.8 %collective-permute-done.9 = f32[8,8,3,128]{3,0,2,1:T(8,128)S(1)} collective-permute-done((f32[8,8,3,128]{3,0,2,1:T(8,128)S(1)}, f32[8,8,3,128]{3,0,2,1:T(8,128)S(1)}, u32[]{:S(2)}, u32[]{:S(2)}) %collective-permute-start.9) | collective-permute-done | bytes 98336 | tf_op jit(solution)/shard_map/ppermute | solution.py:21
  215.9 2.6 gather_fusion.8
  221.3 3.9 %collective-permute-start.10 = (f32[8,8,3,128]{3,0,2,1:T(8,128)S(1)}, f32[8,8,3,128]{3,0,2,1:T(8,128)S(1)}, u32[]{:S(2)}, u32[]{:S(2)}) collective-permute-start(f32[8,8,3,128]{3,0,2,1:T(8,128)S(1)} %slice.154), channel_id=1, source_target_pairs={{4,0},{8,4},{12,8},{16,12},{20,16},{24,20},{28,24},{32,28},{36,32}... | collective-permute-start | bytes 294920 | tf_op jit(solution)/shard_map/ppermute | solution.py:21
  225.2 2.6 collective-permute-done.10
  231.2 8.8 %collective-permute-done.11 = f32[8,8,3,128]{3,0,2,1:T(8,128)S(1)} collective-permute-done((f32[8,8,3,128]{3,0,2,1:T(8,128)S(1)}, f32[8,8,3,128]{3,0,2,1:T(8,128)S(1)}, u32[]{:S(2)}, u32[]{:S(2)}) %collective-permute-start.11) | collective-permute-done | bytes 98336 | tf_op jit(solution)/shard_map/ppermute | solution.py:21
  244.6 3.9 %collective-permute-start.12 = (f32[8,8,3,128]{3,0,2,1:T(8,128)S(1)}, f32[8,8,3,128]{3,0,2,1:T(8,128)S(1)}, u32[]{:S(2)}, u32[]{:S(2)}) collective-permute-start(f32[8,8,3,128]{3,0,2,1:T(8,128)S(1)} %slice.156), channel_id=1, source_target_pairs={{4,0},{8,4},{12,8},{16,12},{20,16},{24,20},{28,24},{32,28},{36,32}... | collective-permute-start | bytes 294920 | tf_op jit(solution)/shard_map/ppermute | solution.py:21
  248.5 2.6 collective-permute-done.12
  254.5 8.8 %collective-permute-done.13 = f32[8,8,3,128]{3,0,2,1:T(8,128)S(1)} collective-permute-done((f32[8,8,3,128]{3,0,2,1:T(8,128)S(1)}, f32[8,8,3,128]{3,0,2,1:T(8,128)S(1)}, u32[]{:S(2)}, u32[]{:S(2)}) %collective-permute-start.13) | collective-permute-done | bytes 98336 | tf_op jit(solution)/shard_map/ppermute | solution.py:21
  264.2 2.6 gather_fusion.12
  269.6 3.9 %collective-permute-start.14 = (f32[8,8,3,128]{3,0,2,1:T(8,128)S(1)}, f32[8,8,3,128]{3,0,2,1:T(8,128)S(1)}, u32[]{:S(2)}, u32[]{:S(2)}) collective-permute-start(f32[8,8,3,128]{3,0,2,1:T(8,128)S(1)} %slice.158), channel_id=1, source_target_pairs={{4,0},{8,4},{12,8},{16,12},{20,16},{24,20},{28,24},{32,28},{36,32}... | collective-permute-start | bytes 294920 | tf_op jit(solution)/shard_map/ppermute | solution.py:21
  273.5 2.6 collective-permute-done.14
  279.5 8.8 %collective-permute-done.15 = f32[8,8,3,128]{3,0,2,1:T(8,128)S(1)} collective-permute-done((f32[8,8,3,128]{3,0,2,1:T(8,128)S(1)}, f32[8,8,3,128]{3,0,2,1:T(8,128)S(1)}, u32[]{:S(2)}, u32[]{:S(2)}) %collective-permute-start.15) | collective-permute-done | bytes 98336 | tf_op jit(solution)/shard_map/ppermute | solution.py:21
  292.9 4.1 %collective-permute-start.16 = (f32[8,8,3,128]{3,0,2,1:T(8,128)S(1)}, f32[8,8,3,128]{3,0,2,1:T(8,128)S(1)}, u32[]{:S(2)}, u32[]{:S(2)}) collective-permute-start(f32[8,8,3,128]{3,0,2,1:T(8,128)S(1)} %slice.160), channel_id=1, source_target_pairs={{4,0},{8,4},{12,8},{16,12},{20,16},{24,20},{28,24},{32,28},{36,32}... | collective-permute-start | bytes 294920 | tf_op jit(solution)/shard_map/ppermute | solution.py:21
  297.0 2.6 collective-permute-done.16
  303.0 8.8 %collective-permute-done.17 = f32[8,8,3,128]{3,0,2,1:T(8,128)S(1)} collective-permute-done((f32[8,8,3,128]{3,0,2,1:T(8,128)S(1)}, f32[8,8,3,128]{3,0,2,1:T(8,128)S(1)}, u32[]{:S(2)}, u32[]{:S(2)}) %collective-permute-start.17) | collective-permute-done | bytes 98336 | tf_op jit(solution)/shard_map/ppermute | solution.py:21
  (182 shorter events, 68.6 us)
Async XLA Ops:
  0.6 117.5 %copy-start = (f32[16,32,64]{2,1,0:T(8,128)S(1)}, f32[16,32,64]{2,1,0:T(8,128)}, u32[]{:S(2)}) copy-start(f32[16,32,64]{2,1,0:T(8,128)} %param.12) | copy-start | bytes 393220
  3.5 3.8 %copy-start.11 = (s32[16,4]{0,1:T(4,128)S(1)}, s32[16,4]{0,1:T(4,128)}, u32[]{:S(2)}) copy-start(s32[16,4]{0,1:T(4,128)} %param.14) | copy-start | bytes 772
  3.5 14.8 %copy-start.1 = (f32[16,32,32]{2,1,0:T(8,128)S(1)}, f32[16,32,32]{2,1,0:T(8,128)}, u32[]{:S(2)}) copy-start(f32[16,32,32]{2,1,0:T(8,128)} %param.13) | copy-start | bytes 196612
  3.5 30.9 %all-to-all-start = ((f32[3,128,1024]{1,0,2:T(4,128)}), f32[3,128,1024]{1,0,2:T(4,128)S(1)}, u32[]{:S(2)}, u32[]{:S(2)}) async-start(f32[3,128,1024]{1,0,2:T(4,128)} %copy.91), calls=%async_computation | async-start | bytes 4194304 | tf_op jit(solution)/shard_map/all_to_all | solution.py:82
  7.7 77.5 %collective-permute-start.2 = (f32[8]{0:T(128)S(1)}, f32[8]{0:T(128)S(1)}, u32[]{:S(2)}, u32[]{:S(2)}) collective-permute-start(f32[8]{0:T(128)S(1)} %slice.93), channel_id=1, source_target_pairs={{4,0},{8,4},{12,8},{16,12},{20,16},{24,20},{28,24},{32,28},{36,32}... | collective-permute-start | bytes 104 | tf_op jit(solution)/shard_map/ppermute | solution.py:21
  19.7 65.7 %collective-permute-start.1 = (f32[8,8]{0,1:T(8,128)S(1)}, f32[8,8]{0,1:T(8,128)S(1)}, u32[]{:S(2)}, u32[]{:S(2)}) collective-permute-start(f32[8,8]{0,1:T(8,128)S(1)} %slice.91), channel_id=1, source_target_pairs={{4,0},{8,4},{12,8},{16,12},{20,16},{24,20},{28,24},{32,28},{36,32}... | collective-permute-start | bytes 776 | tf_op jit(solution)/shard_map/ppermute | solution.py:21
  25.6 1.1 copy-start.8
  26.7 106.8 %copy-start.9 = (s32[1024]{0:T(1024)}, s32[1024]{0:T(1024)S(1)}, u32[]{:S(2)}) copy-start(s32[1024]{0:T(1024)S(1)} %pad_clamp_fusion.1) | copy-start | bytes 12292
  60.3 3.4 %copy-start.4 = (f32[3,512,256]{1,2,0:T(8,128)S(1)}, f32[3,512,256]{1,2,0:T(8,128)}, u32[]{:S(2)}) copy-start(f32[3,512,256]{1,2,0:T(8,128)} %all_to_all.23) | copy-start | bytes 4718596
  63.7 7.3 %copy-start.2 = (f32[3,512,256]{2,1,0:T(8,128)S(1)}, f32[3,512,256]{2,1,0:T(8,128)}, u32[]{:S(2)}) copy-start(f32[3,512,256]{2,1,0:T(8,128)} %copy.95) | copy-start | bytes 4718596
  63.7 7.3 %copy-start.3 = (f32[3,512,256]{2,1,0:T(8,128)S(1)}, f32[3,512,256]{2,1,0:T(8,128)}, u32[]{:S(2)}) copy-start(f32[3,512,256]{2,1,0:T(8,128)} %copy.97) | copy-start | bytes 4718596
  63.7 7.3 %copy-start.6 = (f32[512,256]{1,0:T(8,128)S(1)}, f32[512,256]{1,0:T(8,128)}, u32[]{:S(2)}) copy-start(f32[512,256]{1,0:T(8,128)} %copy.101) | copy-start | bytes 1572868
  63.7 7.3 %copy-start.7 = (f32[512,256]{1,0:T(8,128)S(1)}, f32[512,256]{1,0:T(8,128)}, u32[]{:S(2)}) copy-start(f32[512,256]{1,0:T(8,128)} %copy.93) | copy-start | bytes 1572868
  80.7 31.7 %all-to-all-start.1 = ((f32[3,512,256]{2,0,1:T(4,128)}), f32[3,512,256]{2,0,1:T(4,128)}, u32[]{:S(2)}, u32[]{:S(2)}) async-start(f32[3,512,256]{2,0,1:T(4,128)} %copy.104), calls=%async_computation.1 | async-start | bytes 4194304 | tf_op jit(solution)/shard_map/all_to_all | solution.py:94
  119.9 12.9 %collective-permute-start = (f32[8,8,3,128]{3,0,2,1:T(8,128)S(1)}, f32[8,8,3,128]{3,0,2,1:T(8,128)S(1)}, u32[]{:S(2)}, u32[]{:S(2)}) collective-permute-start(f32[8,8,3,128]{3,0,2,1:T(8,128)S(1)} %slice.146), channel_id=1, source_target_pairs={{4,0},{8,4},{12,8},{16,12},{20,16},{24,20},{28,24},{32,28},{36,32}... | collective-permute-start | bytes 294920 | tf_op jit(solution)/shard_map/ppermute | solution.py:21
  134.2 11.1 %collective-permute-start.3 = (f32[8,8,3,128]{3,0,2,1:T(8,128)S(1)}, f32[8,8,3,128]{3,0,2,1:T(8,128)S(1)}, u32[]{:S(2)}, u32[]{:S(2)}) collective-permute-start(f32[8,8,3,128]{3,0,2,1:T(8,128)S(1)} %copy_select_fusion.7), channel_id=1, source_target_pairs={{0,4},{4,8},{8,12},{12,16},{16,20},{20,24},{24,28},{28,32},{32,36}... | collective-permute-start | bytes 294920 | tf_op jit(solution)/shard_map/ppermute | solution.py:21
  136.1 10.8 %copy-start.10 = (s32[1024]{0:T(1024)}, s32[1024]{0:T(1024)S(1)}, u32[]{:S(2)}) copy-start(s32[1024]{0:T(1024)S(1)} %pad_clamp_fusion) | copy-start | bytes 12292
  149.7 6.5 %collective-permute-start.4 = (f32[8,8,3,128]{3,0,2,1:T(8,128)S(1)}, f32[8,8,3,128]{3,0,2,1:T(8,128)S(1)}, u32[]{:S(2)}, u32[]{:S(2)}) collective-permute-start(f32[8,8,3,128]{3,0,2,1:T(8,128)S(1)} %slice.148), channel_id=1, source_target_pairs={{4,0},{8,4},{12,8},{16,12},{20,16},{24,20},{28,24},{32,28},{36,32}... | collective-permute-start | bytes 294920 | tf_op jit(solution)/shard_map/ppermute | solution.py:21
  157.7 10.7 %collective-permute-start.5 = (f32[8,8,3,128]{3,0,2,1:T(8,128)S(1)}, f32[8,8,3,128]{3,0,2,1:T(8,128)S(1)}, u32[]{:S(2)}, u32[]{:S(2)}) collective-permute-start(f32[8,8,3,128]{3,0,2,1:T(8,128)S(1)} %copy_select_fusion.6), channel_id=1, source_target_pairs={{0,4},{4,8},{8,12},{12,16},{16,20},{20,24},{24,28},{28,32},{32,36}... | collective-permute-start | bytes 294920 | tf_op jit(solution)/shard_map/ppermute | solution.py:21
  173.0 6.5 %collective-permute-start.6 = (f32[8,8,3,128]{3,0,2,1:T(8,128)S(1)}, f32[8,8,3,128]{3,0,2,1:T(8,128)S(1)}, u32[]{:S(2)}, u32[]{:S(2)}) collective-permute-start(f32[8,8,3,128]{3,0,2,1:T(8,128)S(1)} %slice.150), channel_id=1, source_target_pairs={{4,0},{8,4},{12,8},{16,12},{20,16},{24,20},{28,24},{32,28},{36,32}... | collective-permute-start | bytes 294920 | tf_op jit(solution)/shard_map/ppermute | solution.py:21
  181.0 10.7 %collective-permute-start.7 = (f32[8,8,3,128]{3,0,2,1:T(8,128)S(1)}, f32[8,8,3,128]{3,0,2,1:T(8,128)S(1)}, u32[]{:S(2)}, u32[]{:S(2)}) collective-permute-start(f32[8,8,3,128]{3,0,2,1:T(8,128)S(1)} %copy_select_fusion.5), channel_id=1, source_target_pairs={{0,4},{4,8},{8,12},{12,16},{16,20},{20,24},{24,28},{28,32},{32,36}... | collective-permute-start | bytes 294920 | tf_op jit(solution)/shard_map/ppermute | solution.py:21
  196.2 6.5 %collective-permute-start.8 = (f32[8,8,3,128]{3,0,2,1:T(8,128)S(1)}, f32[8,8,3,128]{3,0,2,1:T(8,128)S(1)}, u32[]{:S(2)}, u32[]{:S(2)}) collective-permute-start(f32[8,8,3,128]{3,0,2,1:T(8,128)S(1)} %slice.152), channel_id=1, source_target_pairs={{4,0},{8,4},{12,8},{16,12},{20,16},{24,20},{28,24},{32,28},{36,32}... | collective-permute-start | bytes 294920 | tf_op jit(solution)/shard_map/ppermute | solution.py:21
  204.3 10.7 %collective-permute-start.9 = (f32[8,8,3,128]{3,0,2,1:T(8,128)S(1)}, f32[8,8,3,128]{3,0,2,1:T(8,128)S(1)}, u32[]{:S(2)}, u32[]{:S(2)}) collective-permute-start(f32[8,8,3,128]{3,0,2,1:T(8,128)S(1)} %copy_select_fusion.4), channel_id=1, source_target_pairs={{0,4},{4,8},{8,12},{12,16},{16,20},{20,24},{24,28},{28,32},{32,36}... | collective-permute-start | bytes 294920 | tf_op jit(solution)/shard_map/ppermute | solution.py:21
  221.3 6.5 %collective-permute-start.10 = (f32[8,8,3,128]{3,0,2,1:T(8,128)S(1)}, f32[8,8,3,128]{3,0,2,1:T(8,128)S(1)}, u32[]{:S(2)}, u32[]{:S(2)}) collective-permute-start(f32[8,8,3,128]{3,0,2,1:T(8,128)S(1)} %slice.154), channel_id=1, source_target_pairs={{4,0},{8,4},{12,8},{16,12},{20,16},{24,20},{28,24},{32,28},{36,32}... | collective-permute-start | bytes 294920 | tf_op jit(solution)/shard_map/ppermute | solution.py:21
  229.3 10.7 %collective-permute-start.11 = (f32[8,8,3,128]{3,0,2,1:T(8,128)S(1)}, f32[8,8,3,128]{3,0,2,1:T(8,128)S(1)}, u32[]{:S(2)}, u32[]{:S(2)}) collective-permute-start(f32[8,8,3,128]{3,0,2,1:T(8,128)S(1)} %copy_select_fusion.3), channel_id=1, source_target_pairs={{0,4},{4,8},{8,12},{12,16},{16,20},{20,24},{24,28},{28,32},{32,36}... | collective-permute-start | bytes 294920 | tf_op jit(solution)/shard_map/ppermute | solution.py:21
  244.6 6.5 %collective-permute-start.12 = (f32[8,8,3,128]{3,0,2,1:T(8,128)S(1)}, f32[8,8,3,128]{3,0,2,1:T(8,128)S(1)}, u32[]{:S(2)}, u32[]{:S(2)}) collective-permute-start(f32[8,8,3,128]{3,0,2,1:T(8,128)S(1)} %slice.156), channel_id=1, source_target_pairs={{4,0},{8,4},{12,8},{16,12},{20,16},{24,20},{28,24},{32,28},{36,32}... | collective-permute-start | bytes 294920 | tf_op jit(solution)/shard_map/ppermute | solution.py:21
  252.6 10.7 %collective-permute-start.13 = (f32[8,8,3,128]{3,0,2,1:T(8,128)S(1)}, f32[8,8,3,128]{3,0,2,1:T(8,128)S(1)}, u32[]{:S(2)}, u32[]{:S(2)}) collective-permute-start(f32[8,8,3,128]{3,0,2,1:T(8,128)S(1)} %copy_select_fusion.2), channel_id=1, source_target_pairs={{0,4},{4,8},{8,12},{12,16},{16,20},{20,24},{24,28},{28,32},{32,36}... | collective-permute-start | bytes 294920 | tf_op jit(solution)/shard_map/ppermute | solution.py:21
  269.6 6.5 %collective-permute-start.14 = (f32[8,8,3,128]{3,0,2,1:T(8,128)S(1)}, f32[8,8,3,128]{3,0,2,1:T(8,128)S(1)}, u32[]{:S(2)}, u32[]{:S(2)}) collective-permute-start(f32[8,8,3,128]{3,0,2,1:T(8,128)S(1)} %slice.158), channel_id=1, source_target_pairs={{4,0},{8,4},{12,8},{16,12},{20,16},{24,20},{28,24},{32,28},{36,32}... | collective-permute-start | bytes 294920 | tf_op jit(solution)/shard_map/ppermute | solution.py:21
  277.6 10.7 %collective-permute-start.15 = (f32[8,8,3,128]{3,0,2,1:T(8,128)S(1)}, f32[8,8,3,128]{3,0,2,1:T(8,128)S(1)}, u32[]{:S(2)}, u32[]{:S(2)}) collective-permute-start(f32[8,8,3,128]{3,0,2,1:T(8,128)S(1)} %copy_select_fusion.1), channel_id=1, source_target_pairs={{0,4},{4,8},{8,12},{12,16},{16,20},{20,24},{24,28},{28,32},{32,36}... | collective-permute-start | bytes 294920 | tf_op jit(solution)/shard_map/ppermute | solution.py:21
  292.9 6.7 %collective-permute-start.16 = (f32[8,8,3,128]{3,0,2,1:T(8,128)S(1)}, f32[8,8,3,128]{3,0,2,1:T(8,128)S(1)}, u32[]{:S(2)}, u32[]{:S(2)}) collective-permute-start(f32[8,8,3,128]{3,0,2,1:T(8,128)S(1)} %slice.160), channel_id=1, source_target_pairs={{4,0},{8,4},{12,8},{16,12},{20,16},{24,20},{28,24},{32,28},{36,32}... | collective-permute-start | bytes 294920 | tf_op jit(solution)/shard_map/ppermute | solution.py:21
  300.3 11.5 %copy-start.5 = (f32[32,8,3,128]{3,1,2,0:T(8,128)}, f32[32,8,3,128]{3,1,2,0:T(8,128)S(1)}, u32[]{:S(2)}) copy-start(f32[32,8,3,128]{3,1,2,0:T(8,128)S(1)} %copy.169) | copy-start | bytes 1179652
  301.1 10.7 %collective-permute-start.17 = (f32[8,8,3,128]{3,0,2,1:T(8,128)S(1)}, f32[8,8,3,128]{3,0,2,1:T(8,128)S(1)}, u32[]{:S(2)}, u32[]{:S(2)}) collective-permute-start(f32[8,8,3,128]{3,0,2,1:T(8,128)S(1)} %copy_select_fusion), channel_id=1, source_target_pairs={{0,4},{4,8},{8,12},{12,16},{16,20},{20,24},{24,28},{28,32},{32,36}... | collective-permute-start | bytes 294920 | tf_op jit(solution)/shard_map/ppermute | solution.py:21
where the time goes:
time: 321 us; the launch traced here: 316 us
  waiting for transfers between devices  124 us (39%)
  starting transfers between devices  75.4 us (23%)
  local copies, waits for them, and re-layouts  54 us (17%)
  matrix products  45.6 us (14%)
  other arithmetic  15 us (5%)
    ppermute x18, waiting for transfers between devices, from_behind(): return lax.ppermute(array, axis, pairs)  90.8 us
    ppermute x18, starting transfers between devices, from_behind(): return lax.ppermute(array, axis, pairs)  67.2 us
    all_to_all x1, waiting for transfers between devices, shards(): lax.all_to_all(spectral, 'mode', split_axis=1, concat_axis=2, tiled=True)  26.7 us
    gather x8, local copies, waits for them, and re-layouts, shards(): jnp.take(extended, face_slots, axis=0)  14.1 us
    select_n x9, other arithmetic, shards(): jnp.take(extended, face_slots, axis=0)  8.99 us
    dot_general x1, matrix products, shards(): physical = jnp.einsum('pm,cmq->cpq', basis, coeffs, precision=HIGHEST)  8.22 us
    unnamed x29, local copies, waits for them, and re-layouts  7.9 us
    dot_general x1, matrix products, shards(): spectral = jnp.einsum('pm,cpq->cmq', basis, nonlinear, precision=HIGHEST)  7.89 us
  transfers between devices with their start and end apart: 20, of which 18 were waited for; matrix products, arithmetic and copies ran while one was open for 16% of the time, Pallas kernels for 0%

commit v1 on v0

v1 whole, which is shorter than its diff:
```python
import functools
import math

import jax
import jax.numpy as jnp
import ml_dtypes
import numpy as np
from jax import lax
from jax.experimental import pallas as pl
from jax.experimental.pallas import tpu as pltpu
from jax.sharding import PartitionSpec as P

NODES1 = 8
SWEEPS = 8
TIME_STEP = 0.01
RELAXATION = 0.8
HELMHOLTZ_BASE = 0.5
F32 = jnp.float32
BF16 = jnp.bfloat16
VMEM = pl.BlockSpec(memory_space=pltpu.VMEM)
SMEM = pl.BlockSpec(memory_space=pltpu.SMEM)


def split(x):
    high = x.astype(BF16)
    return high, (x - high.astype(F32)).astype(BF16)


def dot(a, b):
    return jnp.dot(a, b, preferred_element_type=F32)


def np_split(x):
    high = x.astype(np.float32).astype(ml_dtypes.bfloat16)
    low = (x - high.astype(np.float64)).astype(np.float32).astype(ml_dtypes.bfloat16)
    return high, low


def edge_derivative(length):
    index = np.arange(length)
    points_at = np.cos(math.pi * index / (length - 1))
    weights = np.where((index == 0) | (index == length - 1), 2.0, 1.0)
    signs = 1.0 - 2.0 * ((index[:, None] + index[None, :]) % 2)
    same = index[:, None] == index[None, :]
    spacing = np.where(same, 1.0, points_at[:, None] - points_at[None, :])
    offdiag = np.where(same, 0.0, weights[:, None] / weights[None, :] * signs / spacing)
    return offdiag - np.diag(offdiag.sum(axis=1))


def node_table(share):
    edge = edge_derivative(NODES1)
    eye = np.eye(NODES1)
    several = np.eye(share // (NODES1 * NODES1))
    along_r = np.kron(several, np.kron(eye, edge)).T
    along_s = np.kron(several, np.kron(edge, eye)).T
    high, low = np_split(np.concatenate([along_r, along_s], axis=1))
    return np.concatenate([high, high, low], axis=0)


def plane_tables(length):
    plane = np.arange(length)[:, None]
    column = np.arange(length)[None, :]
    wave = (column + 1) // 2
    angle = 2.0 * math.pi / length * (wave * plane % length)
    is_sine = (column % 2 == 0) & (column > 0)
    is_edge = (column == 0) | (column == length - 1)
    factor = np.where(is_edge, math.sqrt(1.0 / length), math.sqrt(2.0 / length))
    rate = wave * (8.0 / length)
    basis = factor * np.where(is_sine, np.sin(angle), np.cos(angle))
    slope = factor * rate * np.where(is_sine, np.cos(angle), -np.sin(angle))
    slope = np.where(column == length - 1, 0.0, slope)
    high, low = np_split(np.concatenate([basis, slope], axis=0))
    forward = np.concatenate([high, high, low], axis=1)
    high, low = np_split(basis.T)
    return forward, np.concatenate([high, high, low], axis=1)


def setup_kernel(info, conn, send, blocks, lift, abb, ai, abi, fh, fl, dgs, dgh, dgi, pos, a, f, dg):
    elem_count, width, node_count = lift.shape
    faces = 2 * elem_count
    halo = send.shape[0]
    edge = 2 * halo * NODES1
    total = a.shape[0]
    for face in range(faces):
        pos[face] = jnp.int32(-1)
    for k in range(halo):
        pos[send[k]] = jnp.int32(k)
    count = jnp.int32(2 * halo)
    for face in range(faces):
        now = pos[face]
        pos[face] = jnp.where(now < 0, count, now)
        count = count + jnp.where(now < 0, 1, 0)
    a[...] = jnp.zeros_like(a)
    f[...] = jnp.zeros_like(f)
    dg[...] = jnp.zeros_like(dg)
    lane = lax.broadcasted_iota(jnp.int32, (NODES1, total), 1)
    sub = lax.broadcasted_iota(jnp.int32, (NODES1, total), 0)
    eye = lax.broadcasted_iota(jnp.int32, (width, width), 0) == lax.broadcasted_iota(
        jnp.int32, (width, width), 1
    )
    first_half = lax.broadcasted_iota(jnp.int32, (width, 128), 1) < 64
    for e in range(elem_count):
        at, live = [], []
        for j in range(4):
            slot = conn[4 * e + j]
            own = slot < faces
            at.append(jnp.where(own, pos[jnp.minimum(slot, faces - 1)], slot - (faces - halo)))
            live.append(jnp.where(own | (info[0] > 0), 1.0, 0.0).astype(F32))
        place = jnp.concatenate(
            [jnp.where(lane == sub + NODES1 * at[j], live[j], 0.0) for j in range(4)], axis=0
        )
        block = blocks[e]
        rows = jnp.dot(block, place, precision=lax.Precision.HIGHEST, preferred_element_type=F32)
        diag = jnp.sum(jnp.where(eye, block, 0.0), axis=1, keepdims=True)
        diag = jnp.where(first_half, jnp.broadcast_to(diag, (width, 128)), 1.0)
        for j in range(4):
            here = pl.ds(pl.multiple_of(NODES1 * at[j], NODES1), NODES1)
            part = slice(NODES1 * j, NODES1 * (j + 1))
            nodes = slice(node_count * e, node_count * (e + 1))
            a[here, :] += live[j] * rows[part]
            dg[here, :] += live[j] * diag[part]
            f[here, nodes] += live[j] * lift[e, part, :]
    high, low = split(a[:edge, :edge])
    abb[...] = jnp.concatenate([high, high, low], axis=1)
    high, low = split(a[edge:, :])
    ai[...] = jnp.concatenate([high, high, low], axis=1)
    high, low = split(a[:edge, edge:])
    abi[...] = jnp.concatenate([high, high, low], axis=1)
    high, low = split(f[...])
    fh[...] = high
    fl[...] = low
    dgs[...] = dg[: edge // 2, :]
    dgh[...] = dg[edge // 2 : edge, :]
    dgi[...] = dg[edge:, :]


def weights_kernel(info, dgs, dgh, dgi, right, left, winv, keep):
    base = info[1] * 128
    wave = (lax.broadcasted_iota(jnp.int32, (1, 128), 1) + base + 1) // 2
    rate = wave.astype(F32) * info[2].astype(F32) ** -1 * 8.0
    kappa = HELMHOLTZ_BASE + rate * rate

    def put(rows, table):
        diag = jnp.broadcast_to(table[:, 0:1], table.shape)
        hits = kappa * jnp.broadcast_to(table[:, 64:65], table.shape)
        inverse = RELAXATION / (diag + hits)
        winv[rows, :] = inverse
        keep[rows, :] = 1.0 - inverse * hits

    half = dgs.shape[0]
    put(slice(0, half), dgs[...] + right[...])
    put(slice(half, 2 * half), dgh[...] + left[...])
    put(slice(2 * half, winv.shape[0]), dgi[...])


def advect_kernel(info, own, one, two, three, metric, forward, back, nodes, o0, o1, o2, o3, c3, n3):
    me = info[1]
    modes, share = own.shape[1], own.shape[2]
    planes = back.shape[0]
    for r, ref in enumerate((own, one, two, three)):
        row = pl.multiple_of((me ^ r) * modes, modes)
        for c in range(3):
            high, low = split(ref[c])
            lanes = slice(c * share, (c + 1) * share)
            c3[pl.ds(row, modes), lanes] = high
            c3[pl.ds(planes + row, modes), lanes] = low
            c3[pl.ds(2 * planes + row, modes), lanes] = high
    here = metric[:, pl.ds(pl.multiple_of(me * share, share), share)]
    rx, sx, ry, sy = (here[k : k + 1, :] for k in range(4))
    step = 128
    for start in range(0, planes, step):
        rows = slice(start, start + step)
        physical = dot(forward[rows, :], c3[...])
        along_z = dot(forward[planes + start : planes + start + step, :], c3[...])
        stacked = jnp.concatenate(
            [physical[:, c * share : (c + 1) * share] for c in range(3)], axis=0
        )
        high, low = split(stacked)
        slopes = dot(jnp.concatenate([high, low, high], axis=1), nodes[...])
        p0, p1, p2 = (physical[:, c * share : (c + 1) * share] for c in range(3))
        for c in range(3):
            lanes = slice(c * share, (c + 1) * share)
            by_r = slopes[c * step : (c + 1) * step, :share]
            by_s = slopes[c * step : (c + 1) * step, share:]
            term = p0 * (rx * by_r + sx * by_s) + p1 * (ry * by_r + sy * by_s)
            term = term + p2 * along_z[:, lanes]
            high, low = split(term)
            n3[start : start + step, lanes] = high
            n3[planes + start : planes + start + step, lanes] = low
            n3[2 * planes + start : 2 * planes + start + step, lanes] = high
    for r, ref in ((2, o2), (3, o3), (1, o1), (0, o0)):
        row = pl.multiple_of((me ^ r) * modes, modes)
        spectral = dot(back[pl.ds(row, modes), :], n3[...])
        for c in range(3):
            ref[c] = spectral[:, c * share : (c + 1) * share]


def triple(x):
    return jnp.concatenate([x, x, x], axis=1)


def stack(x):
    high, low = split(x)
    return jnp.concatenate([high, low, high], axis=0)


def forcing_kernel(info, velocity, own, one, two, three, fh, fl, winv, abi, rhs, fs, fi_w, fhalo, pib):
    me = info[1]
    share = own.shape[2]
    for r, ref in enumerate((own, one, two, three)):
        lanes = pl.ds(pl.multiple_of((me ^ r) * share, share), share)
        for c in range(3):
            rhs[c, :, lanes] = velocity[c, :, lanes] - TIME_STEP * ref[c]
    half = fs.shape[0]
    modes = rhs.shape[1]
    for c in range(3):
        high, low = split(rhs[c])
        nt = (((1,), (1,)), ((), ()))
        force = lax.dot_general(fh[...], high, nt, preferred_element_type=F32)
        force += lax.dot_general(fh[...], low, nt, preferred_element_type=F32)
        force += lax.dot_general(fl[...], high, nt, preferred_element_type=F32)
        lanes = slice(c * modes, (c + 1) * modes)
        fs[:, lanes] = force[:half]
        fhalo[:, lanes] = force[half : 2 * half]
        fi_w[:, lanes] = winv[2 * half :, :] * force[2 * half :]
    pib[...] = dot(abi[...], stack(fi_w[...]))


def first_kernel(fs, fhalo, right, left, winv, pib, abb, wfb, tb, ps, ph):
    half = fs.shape[0]
    force = jnp.concatenate([fs[...] + right[...], fhalo[...] + left[...]], axis=0)
    now = triple(winv[: 2 * half, :]) * force
    wfb[...] = now
    tb[...] = now
    out = dot(abb[...], stack(now)) + pib[...]
    ps[...] = out[:half]
    ph[...] = out[half:]


def edge_update(ps, ph, right, left, tb, winv, keep, wfb):
    half = ps.shape[0]
    product = jnp.concatenate([ps[...] + right[...], ph[...] + left[...]], axis=0)
    scale = triple(winv[: 2 * half, :])
    return triple(keep[: 2 * half, :]) * tb[...] + wfb[...] - scale * product


def edge_kernel(ps, ph, right, left, tb, winv, keep, wfb, pib, abb, tb_out, ps_out, ph_out):
    half = ps.shape[0]
    now = edge_update(ps, ph, right, left, tb, winv, keep, wfb)
    tb_out[...] = now
    out = dot(abb[...], stack(now)) + pib[...]
    ps_out[...] = out[:half]
    ph_out[...] = out[half:]


def inner_kernel(tb, ti, winv, keep, wfi, ai, abi, ti_out, pib_out):
    edge = tb.shape[0]
    product = dot(ai[...], stack(jnp.concatenate([tb[...], ti[...]], axis=0)))
    now = triple(keep[edge:, :]) * ti[...] + wfi[...] - triple(winv[edge:, :]) * product
    ti_out[...] = now
    pib_out[...] = dot(abi[...], stack(now))


def final_kernel(pos, ps, ph, right, left, tb, winv, keep, wfb, ti, rhs, fh, fl, out, trace, t):
    edge = tb.shape[0]
    modes = rhs.shape[1]
    t[:edge, :] = edge_update(ps, ph, right, left, tb, winv, keep, wfb)
    t[edge:, :] = ti[...]
    for face in range(trace.shape[0] // NODES1):
        row = pl.multiple_of(pos[face] * NODES1, NODES1)
        trace[face * NODES1 : (face + 1) * NODES1, :] = t[pl.ds(row, NODES1), :]
    for c in range(3):
        high, low = split(t[:, c * modes : (c + 1) * modes].T)
        add = dot(high, fh[...]) + dot(low, fh[...]) + dot(high, fl[...])
        out[c] = rhs[c] + add


def call(kernel, outs, *args, smem=(), smem_out=(), scratch=(), flops=0, limit=32):
    size = sum(x.size * x.dtype.itemsize for x in (*args, *outs))
    return pl.pallas_call(
        kernel,
        out_shape=tuple(outs),
        in_specs=[SMEM if k in smem else VMEM for k in range(len(args))],
        out_specs=tuple(SMEM if k in smem_out else VMEM for k in range(len(outs))),
        scratch_shapes=list(scratch),
        cost_estimate=pl.CostEstimate(flops=int(flops), bytes_accessed=int(size), transcendentals=0),
        compiler_params=pltpu.CompilerParams(vmem_limit_bytes=limit * 2**20),
    )(*args)


def arr(*shape, dtype=F32):
    return jax.ShapeDtypeStruct(shape, dtype)


def shards(velocity, metric, lift, blocks, conn, send_list):
    modes, points = velocity.shape[1:]
    ways = lax.axis_size("mode")
    planes = modes * ways
    share = points // ways
    elem_count = lift.shape[0]
    faces = 2 * elem_count
    halo = send_list.shape[1]
    half = halo * NODES1
    edge = 2 * half
    total = (faces + halo) * NODES1
    inner = total - edge
    cols = 3 * modes
    me = lax.axis_index("mode")
    part = lax.axis_index("elem")
    count = lax.axis_size("elem")
    ring = [(i, (i + 1) % count) for i in range(count)]
    back_ring = [(j, i) for i, j in ring]
    info = jnp.stack([part, me, jnp.int32(planes)]).astype(jnp.int32)

    def swap(x, r):
        return lax.ppermute(x, "mode", [(j, j ^ r) for j in range(ways)])

    def exchange(to_right, to_left):
        left = lax.ppermute(to_right, "elem", ring)
        right = lax.ppermute(to_left, "elem", back_ring)
        return right, left

    pieces = [lax.dynamic_slice_in_dim(velocity, (me ^ r) * share, share, 2) for r in range(ways)]
    got = {r: swap(pieces[r], r) for r in (2, 3, 1)}

    abb, ai, abi, fh, fl, dgs, dgh, dgi, pos = call(
        setup_kernel,
        [
            arr(edge, 3 * edge, dtype=BF16),
            arr(inner, 3 * total, dtype=BF16),
            arr(edge, 3 * inner, dtype=BF16),
            arr(total, points, dtype=BF16),
            arr(total, points, dtype=BF16),
            arr(half, 128),
            arr(half, 128),
            arr(inner, 128),
            arr(faces, dtype=jnp.int32),
        ],
        info,
        conn.reshape(-1),
        send_list.reshape(-1),
        blocks,
        lift,
        smem=(0, 1, 2),
        smem_out=(8,),
        scratch=[pltpu.VMEM((total, total), F32), pltpu.VMEM((total, points), F32), pltpu.VMEM((total, 128), F32)],
        flops=1e8,
    )
    right, left = exchange(dgs, dgh)
    winv, keep = call(
        weights_kernel, [arr(total, 128), arr(total, 128)], info, dgs, dgh, dgi, right, left, smem=(0,)
    )

    forward, back = plane_tables(planes)
    nodes = node_table(share)
    quarter = arr(3, modes, share)
    outs = call(
        advect_kernel,
        [quarter] * 4,
        info,
        pieces[0],
        got[1],
        got[2],
        got[3],
        metric,
        jnp.asarray(forward),
        jnp.asarray(back),
        jnp.asarray(nodes),
        smem=(0,),
        scratch=[pltpu.VMEM((3 * planes, 3 * share), BF16), pltpu.VMEM((3 * planes, 3 * share), BF16)],
        flops=5e9,
    )
    home = {r: swap(outs[r], r) for r in (2, 3, 1)}
    rhs, fs, wfi, fhalo, pib = call(
        forcing_kernel,
        [arr(3, modes, points), arr(half, cols), arr(inner, cols), arr(half, cols), arr(edge, cols)],
        info,
        velocity,
        outs[0],
        home[1],
        home[2],
        home[3],
        fh,
        fl,
        winv,
        abi,
        smem=(0,),
        flops=1e9,
    )
    right, left = exchange(fs, fhalo)
    edge_outs = [arr(edge, cols), arr(half, cols), arr(half, cols)]
    wfb, tb, ps, ph = call(
        first_kernel, [arr(edge, cols)] + edge_outs, fs, fhalo, right, left, winv, pib, abb, flops=1e8, limit=8
    )
    ti = wfi
    for sweep in range(2, SWEEPS + 1):
        right, left = exchange(ps, ph)
        ti, pib = call(
            inner_kernel,
            [arr(inner, cols), arr(edge, cols)],
            tb, ti, winv, keep, wfi, ai, abi,
            flops=3e8,
            limit=8,
        )
        if sweep < SWEEPS:
            tb, ps, ph = call(
                edge_kernel, edge_outs, ps, ph, right, left, tb, winv, keep, wfb, pib, abb, flops=1e8, limit=8
            )
    velocity_new, trace = call(
        final_kernel,
        [arr(3, modes, points), arr(faces * NODES1, cols)],
        pos, ps, ph, right, left, tb, winv, keep, wfb, ti, rhs, fh, fl,
        smem=(0,),
        scratch=[pltpu.VMEM((total, cols), F32)],
        flops=1e9,
    )
    return velocity_new, trace.reshape(faces, NODES1, 3, modes)


def solution(mesh):
    return jax.shard_map(
        shards,
        mesh=mesh,
        in_specs=(
            P(None, "mode", "elem"),
            P(None, "elem"),
            P("elem", None, None),
            P("elem", None, None),
            P("elem", None),
            P("elem", None),
        ),
        out_specs=(P(None, "mode", "elem"), P("elem", None, None, "mode")),
        check_vma=False,
    )
```

time: 321 us -> 142 us (0.44); the launches traced: 316 us -> 141 us
  waiting for transfers between devices: 124 us -> 39.2 us
  matrix products: 45.6 us -> 0 us
  local copies, waits for them, and re-layouts: 54 us -> 8.85 us
  Pallas kernels: 0 us -> 22.7 us
  other arithmetic: 15 us -> 0.08 us
  starting transfers between devices: 75.4 us -> 69.1 us
    ppermute x18 -> x24, waiting for transfers between devices: 90.8 us -> 39.2 us  [the longest x6 22.1 us: swap(): return lax.ppermute(x, 'mode', [(j, j ^ r) for j in range(ways)])]
    dot_general x33 -> x0, matrix products: 45.6 us -> none  [the longest x1 8.22 us: shards(): physical = jnp.einsum('pm,cmq->cpq', basis, coeffs, precision=HIGHEST)]
    all_to_all x2 -> x0, waiting for transfers between devices: 33.5 us -> none  [the longest x1 26.7 us: shards(): lax.all_to_all(spectral, 'mode', split_axis=1, concat_axis=2, tiled=True)]
    pallas_call x0 -> x19, Pallas kernels: none -> 22.7 us  [call(): pl.pallas_call(kernel, out_shape=tuple(outs), in_specs=[SMEM if k in smem...]
    gather x18 -> x0, local copies, waits for them, and re-layouts: 20.2 us -> none  [the longest x8 14.1 us: shards(): jnp.take(extended, face_slots, axis=0)]
    select_n x20 -> x0, other arithmetic: 9.67 us -> none  [the longest x9 8.99 us: shards(): jnp.take(extended, face_slots, axis=0)]
    all_to_all x2 -> x0, starting transfers between devices: 8.18 us -> none  [the longest x1 4.45 us: shards(): lax.all_to_all(spectral, 'mode', split_axis=1, concat_axis=2, tiled=True)]
    mul x9 -> x0, local copies, waits for them, and re-layouts: 6.38 us -> none  [the longest x1 2.17 us: shards(): physical[2] * along_z]
  transfers between devices with their start and end apart: 20 -> 24, of which waited for: 18 -> 12; matrix products, arithmetic and copies ran while one was open for 16% -> 0% of each run, Pallas kernels for 0% -> 6%
where the time goes in v1:
time: 142 us; the launch traced here: 141 us
  starting transfers between devices  69.1 us (49%)
  waiting for transfers between devices  39.2 us (28%)
  Pallas kernels  22.7 us (16%)
  local copies, waits for them, and re-layouts  8.85 us (6%)
    ppermute x9, starting transfers between devices, exchange(): right = lax.ppermute(to_left, 'elem', back_ring)  59.2 us
    pallas_call x19, Pallas kernels, call(): pl.pallas_call(kernel, out_shape=tuple(outs), in_specs=[SMEM if k in smem...  22.7 us
    ppermute x6, waiting for transfers between devices, swap(): return lax.ppermute(x, 'mode', [(j, j ^ r) for j in range(ways)])  22.1 us
    ppermute x9, waiting for transfers between devices, exchange(): left = lax.ppermute(to_right, 'elem', ring)  17.1 us
    unnamed x23, local copies, waits for them, and re-layouts  7.22 us
    ppermute x6, starting transfers between devices, swap(): return lax.ppermute(x, 'mode', [(j, j ^ r) for j in range(ways)])  6.83 us
    ppermute x9, starting transfers between devices, exchange(): left = lax.ppermute(to_right, 'elem', ring)  3.02 us
  transfers between devices with their start and end apart: 24, of which 12 were waited for; matrix products, arithmetic and copies ran while one was open for 0% of the time, Pallas kernels for 6%

profile of v1, /device:TPU:8, one launch (start us, length us, event | category | flops | bytes accessed | tf_op | source)
XLA Modules:
  0.0 140.7 jit_solution(3323682491315015151)
XLA Ops:
  0.7 1.5 %constant_dynamic-slice_fusion = (f32[3,128,256]{2,1,0:T(8,128)S(1)}, f32[3,128,256]{2,1,0:T(8,128)S(1)}, f32[3,128,256]{2,1,0:T(8,128)S(1)}, f32[3,128,256]{2,1,0:T(8,128)S(1)}) fusion(f32[3,128,1024]{2,1,0:T(8,128)} %velocity.1, s32[]{:T(128)S(6)} %select_n.15, s32[]{:T(128)S(6)} %select_n.14, s32[]{:T(128)S(6)} %select_n.13, s32[]{:T(128)S(6)} %select_n.12), kind=kLoop, calls=%fused_computation | loop fusion | bytes 3145744 | tf_op jit(solution)/shard_map/dynamic_slice | solution.py:323
  2.2 1.8 %collective-permute-start.2 = (f32[3,128,256]{2,1,0:T(8,128)S(1)}, f32[3,128,256]{2,1,0:T(8,128)S(1)}, u32[]{:S(2)}, u32[]{:S(2)}) collective-permute-start(f32[3,128,256]{2,1,0:T(8,128)S(1)} %get-tuple-element.116), channel_id=1, source_target_pairs={{0,3},{1,2},{2,1},{3,0},{4,7},{5,6},{6,5},{7,4},{8,11},{9,10},{10,... | collective-permute-start | bytes 1179656 | tf_op jit(solution)/shard_map/ppermute | solution.py:316
  4.0 1.2 collective-permute-start.1
  5.3 0.4 collective-permute-start
  5.7 9.5 %collective-permute-done.2.three = f32[3,128,256]{2,1,0:T(8,128)S(1)} collective-permute-done((f32[3,128,256]{2,1,0:T(8,128)S(1)}, f32[3,128,256]{2,1,0:T(8,128)S(1)}, u32[]{:S(2)}, u32[]{:S(2)}) %collective-permute-start.2) | collective-permute-done | bytes 393248 | tf_op jit(solution)/shard_map/ppermute | solution.py:316
  15.2 8.4 %collective-permute-done.1.two = f32[3,128,256]{2,1,0:T(8,128)S(1)} collective-permute-done((f32[3,128,256]{2,1,0:T(8,128)S(1)}, f32[3,128,256]{2,1,0:T(8,128)S(1)}, u32[]{:S(2)}, u32[]{:S(2)}) %collective-permute-start.1) | collective-permute-done | bytes 393248 | tf_op jit(solution)/shard_map/ppermute | solution.py:316
  23.7 0.7 copy-done.4
  24.4 1.0 copy-done.5
  25.4 1.9 %copy-done.7 = bf16[1024,1536]{1,0:T(8,128)(2,1)S(1)} copy-done((bf16[1024,1536]{1,0:T(8,128)(2,1)S(1)}, bf16[1024,1536]{1,0:T(8,128)(2,1)}, u32[]{:S(2)}) %copy-start.7) | copy-done | bytes 3145752
  27.3 1.4 copy-done.8
  28.7 1.1 copy-done.9
  29.8 6.7 %shard_map.105 = (f32[3,128,256]{2,1,0:T(8,128)S(1)}, f32[3,128,256]{2,1,0:T(8,128)}, f32[3,128,256]{2,1,0:T(8,128)}, f32[3,128,256]{2,1,0:T(8,128)}) custom-call(s32[3]{0:T(128)S(1)} %pad_add_fusion.info, f32[3,128,256]{2,1,0:T(8,128)S(1)} %get-tuple-element.119.own, f32[3,128,256]{2,1,0:T(8,128)S(1)} %copy-done.5, ...), custom_call_target="tpu_custom_call" | custom-call | flops 5000000000 | bytes 8667148 | tf_op jit(solution)/shard_map/pallas_call | solution.py:280
  36.6 2.3 %collective-permute-start.4 = (f32[3,128,256]{2,1,0:T(8,128)}, f32[3,128,256]{2,1,0:T(8,128)S(1)}, u32[]{:S(2)}, u32[]{:S(2)}) collective-permute-start(f32[3,128,256]{2,1,0:T(8,128)} %get-tuple-element.62), channel_id=1, source_target_pairs={{0,2},{1,3},{2,0},{3,1},{4,6},{5,7},{6,4},{7,5},{8,10},{9,11},{10,... | collective-permute-start | bytes 1179656 | tf_op jit(solution)/shard_map/ppermute | solution.py:316
  38.9 1.0 collective-permute-start.5
  40.1 0.9 copy-done.2
  41.0 2.6 %shard_map.104 = (bf16[128,384]{1,0:T(8,128)(2,1)S(1)}, bf16[192,960]{1,0:T(8,128)(2,1)S(1)}, bf16[128,576]{1,0:T(8,128)(2,1)S(1)}, bf16[320,1024]{1,0:T(8,128)(...) custom-call(s32[3]{0:T(128)S(1)} %pad_add_fusion.info, ...), custom_call_target="tpu_custom_call" | custom-call | flops 100000000 | bytes 2285996 | tf_op jit(solution)/shard_map/pallas_call | solution.py:280
  43.6 1.6 %collective-permute-start.7 = (f32[64,128]{1,0:T(8,128)S(1)}, f32[64,128]{1,0:T(8,128)S(1)}, u32[]{:S(2)}, u32[]{:S(2)}) collective-permute-start(f32[64,128]{1,0:T(8,128)S(1)} %get-tuple-element.66.dgs), channel_id=1, source_target_pairs={{0,4},{4,8},{8,12},{12,16},{16,20},{20,24},{24,28},{28,32},{32,36}... | collective-permute-start | bytes 98312 | tf_op jit(solution)/shard_map/ppermute | solution.py:319
  45.2 6.7 %collective-permute-start.6 = (f32[64,128]{1,0:T(8,128)S(1)}, f32[64,128]{1,0:T(8,128)S(1)}, u32[]{:S(2)}, u32[]{:S(2)}) collective-permute-start(f32[64,128]{1,0:T(8,128)S(1)} %get-tuple-element.67.dgh), channel_id=1, source_target_pairs={{4,0},{8,4},{12,8},{16,12},{20,16},{24,20},{28,24},{32,28},{36,32}... | collective-permute-start | bytes 98312 | tf_op jit(solution)/shard_map/ppermute | solution.py:320
  51.9 1.7 %collective-permute-done.7.left = f32[64,128]{1,0:T(8,128)S(1)} collective-permute-done((f32[64,128]{1,0:T(8,128)S(1)}, f32[64,128]{1,0:T(8,128)S(1)}, u32[]{:S(2)}, u32[]{:S(2)}) %collective-permute-start.7) | collective-permute-done | bytes 32800 | tf_op jit(solution)/shard_map/ppermute | solution.py:319
  53.5 0.7 shard_map.106
  54.3 4.1 %collective-permute-done.5.three = f32[3,128,256]{2,1,0:T(8,128)S(1)} collective-permute-done((f32[3,128,256]{2,1,0:T(8,128)}, f32[3,128,256]{2,1,0:T(8,128)S(1)}, u32[]{:S(2)}, u32[]{:S(2)}) %collective-permute-start.5) | collective-permute-done | bytes 393248 | tf_op jit(solution)/shard_map/ppermute | solution.py:316
  58.4 2.7 %shard_map.107 = (f32[3,128,1024]{2,1,0:T(8,128)S(1)}, f32[64,384]{1,0:T(8,128)S(1)}, f32[192,384]{1,0:T(8,128)S(1)}, f32[64,384]{1,0:T(8,128)S(1)}, f32[128,384]{1,0:T(8,128)S(1)}) custom-call(s32[3]{0:T(128)S(1)} %pad_add_fusion.info, f32[3,128,1024]{2,1,0:T(8,128)S(1)} %copy-done, f32[3,128,256]{2,1,0:T(8,128)S(1)} %get-tuple-element.60.own, ...), custom_call_target="tpu_custom_call" | custom-call | flops 1000000000 | bytes 7028748 | tf_op jit(solution)/shard_map/pallas_call | solution.py:280
  61.2 0.9 collective-permute-start.9
  62.1 7.3 %collective-permute-start.8 = (f32[64,384]{1,0:T(8,128)S(1)}, f32[64,384]{1,0:T(8,128)S(1)}, u32[]{:S(2)}, u32[]{:S(2)}) collective-permute-start(f32[64,384]{1,0:T(8,128)S(1)} %get-tuple-element.72.fhalo), channel_id=1, source_target_pairs={{4,0},{8,4},{12,8},{16,12},{20,16},{24,20},{28,24},{32,28},{36,32}... | collective-permute-start | bytes 294920 | tf_op jit(solution)/shard_map/ppermute | solution.py:320
  69.3 3.1 %collective-permute-done.9.left = f32[64,384]{1,0:T(8,128)S(1)} collective-permute-done((f32[64,384]{1,0:T(8,128)S(1)}, f32[64,384]{1,0:T(8,128)S(1)}, u32[]{:S(2)}, u32[]{:S(2)}) %collective-permute-start.9) | collective-permute-done | bytes 98336 | tf_op jit(solution)/shard_map/ppermute | solution.py:319
  72.7 6.2 %collective-permute-start.10 = (f32[64,384]{1,0:T(8,128)S(1)}, f32[64,384]{1,0:T(8,128)S(1)}, u32[]{:S(2)}, u32[]{:S(2)}) collective-permute-start(f32[64,384]{1,0:T(8,128)S(1)} %get-tuple-element.76.ph), channel_id=1, source_target_pairs={{4,0},{8,4},{12,8},{16,12},{20,16},{24,20},{28,24},{32,28},{36,32}... | collective-permute-start | bytes 294920 | tf_op jit(solution)/shard_map/ppermute | solution.py:320
  79.0 0.6 shard_map.109
  79.6 2.0 %collective-permute-done.11.left = f32[64,384]{1,0:T(8,128)S(1)} collective-permute-done((f32[64,384]{1,0:T(8,128)S(1)}, f32[64,384]{1,0:T(8,128)S(1)}, u32[]{:S(2)}, u32[]{:S(2)}) %collective-permute-start.11) | collective-permute-done | bytes 98336 | tf_op jit(solution)/shard_map/ppermute | solution.py:319
  81.9 6.3 %collective-permute-start.12 = (f32[64,384]{1,0:T(8,128)S(1)}, f32[64,384]{1,0:T(8,128)S(1)}, u32[]{:S(2)}, u32[]{:S(2)}) collective-permute-start(f32[64,384]{1,0:T(8,128)S(1)} %get-tuple-element.84.ph), channel_id=1, source_target_pairs={{4,0},{8,4},{12,8},{16,12},{20,16},{24,20},{28,24},{32,28},{36,32}... | collective-permute-start | bytes 294920 | tf_op jit(solution)/shard_map/ppermute | solution.py:320
  88.2 0.6 shard_map.111
  88.9 1.9 %collective-permute-done.13.left = f32[64,384]{1,0:T(8,128)S(1)} collective-permute-done((f32[64,384]{1,0:T(8,128)S(1)}, f32[64,384]{1,0:T(8,128)S(1)}, u32[]{:S(2)}, u32[]{:S(2)}) %collective-permute-start.13) | collective-permute-done | bytes 98336 | tf_op jit(solution)/shard_map/ppermute | solution.py:319
  90.7 0.3 shard_map.112
  91.1 6.4 %collective-permute-start.14 = (f32[64,384]{1,0:T(8,128)S(1)}, f32[64,384]{1,0:T(8,128)S(1)}, u32[]{:S(2)}, u32[]{:S(2)}) collective-permute-start(f32[64,384]{1,0:T(8,128)S(1)} %get-tuple-element.89.ph), channel_id=1, source_target_pairs={{4,0},{8,4},{12,8},{16,12},{20,16},{24,20},{28,24},{32,28},{36,32}... | collective-permute-start | bytes 294920 | tf_op jit(solution)/shard_map/ppermute | solution.py:320
  97.5 0.6 shard_map.113
  98.1 1.9 %collective-permute-done.15.left = f32[64,384]{1,0:T(8,128)S(1)} collective-permute-done((f32[64,384]{1,0:T(8,128)S(1)}, f32[64,384]{1,0:T(8,128)S(1)}, u32[]{:S(2)}, u32[]{:S(2)}) %collective-permute-start.15) | collective-permute-done | bytes 98336 | tf_op jit(solution)/shard_map/ppermute | solution.py:319
  100.4 6.6 %collective-permute-start.16 = (f32[64,384]{1,0:T(8,128)S(1)}, f32[64,384]{1,0:T(8,128)S(1)}, u32[]{:S(2)}, u32[]{:S(2)}) collective-permute-start(f32[64,384]{1,0:T(8,128)S(1)} %get-tuple-element.94.ph), channel_id=1, source_target_pairs={{4,0},{8,4},{12,8},{16,12},{20,16},{24,20},{28,24},{32,28},{36,32}... | collective-permute-start | bytes 294920 | tf_op jit(solution)/shard_map/ppermute | solution.py:320
  107.0 0.6 shard_map.115
  107.6 1.7 %collective-permute-done.17.left = f32[64,384]{1,0:T(8,128)S(1)} collective-permute-done((f32[64,384]{1,0:T(8,128)S(1)}, f32[64,384]{1,0:T(8,128)S(1)}, u32[]{:S(2)}, u32[]{:S(2)}) %collective-permute-start.17) | collective-permute-done | bytes 98336 | tf_op jit(solution)/shard_map/ppermute | solution.py:319
  109.6 6.6 %collective-permute-start.18 = (f32[64,384]{1,0:T(8,128)S(1)}, f32[64,384]{1,0:T(8,128)S(1)}, u32[]{:S(2)}, u32[]{:S(2)}) collective-permute-start(f32[64,384]{1,0:T(8,128)S(1)} %get-tuple-element.99.ph), channel_id=1, source_target_pairs={{4,0},{8,4},{12,8},{16,12},{20,16},{24,20},{28,24},{32,28},{36,32}... | collective-permute-start | bytes 294920 | tf_op jit(solution)/shard_map/ppermute | solution.py:320
  116.2 0.6 shard_map.117
  116.9 1.9 %collective-permute-done.19.left = f32[64,384]{1,0:T(8,128)S(1)} collective-permute-done((f32[64,384]{1,0:T(8,128)S(1)}, f32[64,384]{1,0:T(8,128)S(1)}, u32[]{:S(2)}, u32[]{:S(2)}) %collective-permute-start.19) | collective-permute-done | bytes 98336 | tf_op jit(solution)/shard_map/ppermute | solution.py:319
  119.1 6.4 %collective-permute-start.20 = (f32[64,384]{1,0:T(8,128)S(1)}, f32[64,384]{1,0:T(8,128)S(1)}, u32[]{:S(2)}, u32[]{:S(2)}) collective-permute-start(f32[64,384]{1,0:T(8,128)S(1)} %get-tuple-element.104.ph), channel_id=1, source_target_pairs={{4,0},{8,4},{12,8},{16,12},{20,16},{24,20},{28,24},{32,28},{36,32}... | collective-permute-start | bytes 294920 | tf_op jit(solution)/shard_map/ppermute | solution.py:320
  125.5 0.6 shard_map.119
  126.1 1.9 %collective-permute-done.21.left = f32[64,384]{1,0:T(8,128)S(1)} collective-permute-done((f32[64,384]{1,0:T(8,128)S(1)}, f32[64,384]{1,0:T(8,128)S(1)}, u32[]{:S(2)}, u32[]{:S(2)}) %collective-permute-start.21) | collective-permute-done | bytes 98336 | tf_op jit(solution)/shard_map/ppermute | solution.py:319
  128.3 6.7 %collective-permute-start.22 = (f32[64,384]{1,0:T(8,128)S(1)}, f32[64,384]{1,0:T(8,128)S(1)}, u32[]{:S(2)}, u32[]{:S(2)}) collective-permute-start(f32[64,384]{1,0:T(8,128)S(1)} %get-tuple-element.109.ph), channel_id=1, source_target_pairs={{4,0},{8,4},{12,8},{16,12},{20,16},{24,20},{28,24},{32,28},{36,32}... | collective-permute-start | bytes 294920 | tf_op jit(solution)/shard_map/ppermute | solution.py:320
  135.0 1.3 shard_map.121
  136.3 1.2 collective-permute-done.23.left
  137.5 3.2 %shard_map.122 = (f32[3,128,1024]{2,1,0:T(8,128)}, f32[256,384]{1,0:T(8,128)}) custom-call(s32[32]{0:T(128)S(1)} %get-tuple-element.59.pos, f32[64,384]{1,0:T(8,128)S(1)} %get-tuple-element.108.ps, f32[64,384]{1,0:T(8,128)S(1)} %get-tuple-element.109.ph, f32[64,384]{1,0:T(8,128)S(1)} %collective-permute-done.22.right, ...), custom_call_target="tpu_custom_call" | custom-call | flops 1000000000 | bytes 6258816 | tf_op jit(solution)/shard_map/pallas_call | solution.py:280
  (45 shorter events, 2.4 us)
Async XLA Ops:
  0.7 23.7 %copy-start.6 = (f32[4,1024]{1,0:T(4,128)S(1)}, f32[4,1024]{1,0:T(4,128)}, u32[]{:S(2)}) copy-start(f32[4,1024]{1,0:T(4,128)} %metric.1) | copy-start | bytes 49156
  2.2 13.0 %collective-permute-start.2 = (f32[3,128,256]{2,1,0:T(8,128)S(1)}, f32[3,128,256]{2,1,0:T(8,128)S(1)}, u32[]{:S(2)}, u32[]{:S(2)}) collective-permute-start(f32[3,128,256]{2,1,0:T(8,128)S(1)} %get-tuple-element.116), channel_id=1, source_target_pairs={{0,3},{1,2},{2,1},{3,0},{4,7},{5,6},{6,5},{7,4},{8,11},{9,10},{10,... | collective-permute-start | bytes 1179656 | tf_op jit(solution)/shard_map/ppermute | solution.py:316
  4.0 19.6 %collective-permute-start.1 = (f32[3,128,256]{2,1,0:T(8,128)S(1)}, f32[3,128,256]{2,1,0:T(8,128)S(1)}, u32[]{:S(2)}, u32[]{:S(2)}) collective-permute-start(f32[3,128,256]{2,1,0:T(8,128)S(1)} %get-tuple-element.117), channel_id=1, source_target_pairs={{0,2},{1,3},{2,0},{3,1},{4,6},{5,7},{6,4},{7,5},{8,10},{9,11},{10,... | collective-permute-start | bytes 1179656 | tf_op jit(solution)/shard_map/ppermute | solution.py:316
  5.3 18.4 %collective-permute-start = (f32[3,128,256]{2,1,0:T(8,128)S(1)}, f32[3,128,256]{2,1,0:T(8,128)S(1)}, u32[]{:S(2)}, u32[]{:S(2)}) collective-permute-start(f32[3,128,256]{2,1,0:T(8,128)S(1)} %get-tuple-element.118), channel_id=1, source_target_pairs={{0,1},{1,0},{2,3},{3,2},{4,5},{5,4},{6,7},{7,6},{8,9},{9,8},{10,11... | collective-permute-start | bytes 1179656 | tf_op jit(solution)/shard_map/ppermute | solution.py:316
  23.7 0.7 copy-start.4
  24.4 1.0 copy-start.5
  25.4 1.9 %copy-start.7 = (bf16[1024,1536]{1,0:T(8,128)(2,1)S(1)}, bf16[1024,1536]{1,0:T(8,128)(2,1)}, u32[]{:S(2)}) copy-start(bf16[1024,1536]{1,0:T(8,128)(2,1)} %constant.29.clone.forward) | copy-start | bytes 9437188
  27.3 1.4 %copy-start.8 = (bf16[512,1536]{1,0:T(8,128)(2,1)S(1)}, bf16[512,1536]{1,0:T(8,128)(2,1)}, u32[]{:S(2)}) copy-start(bf16[512,1536]{1,0:T(8,128)(2,1)} %constant.30.clone.back) | copy-start | bytes 4718596
  28.7 1.1 copy-start.9
  29.8 10.0 %copy-start.10 = (s32[16,4]{0,1:T(4,128)S(1)}, s32[16,4]{0,1:T(4,128)}, u32[]{:S(2)}) copy-start(s32[16,4]{0,1:T(4,128)} %param.13) | copy-start | bytes 772
  29.8 10.2 %copy-start.1 = (f32[16,32,32]{2,1,0:T(8,128)S(1)}, f32[16,32,32]{2,1,0:T(8,128)}, u32[]{:S(2)}) copy-start(f32[16,32,32]{2,1,0:T(8,128)} %blocks.1) | copy-start | bytes 196612
  29.8 10.2 %copy-start.3 = (s32[1,8]{1,0:T(1,128)S(1)}, s32[1,8]{1,0:T(1,128)}, u32[]{:S(2)}) copy-start(s32[1,8]{1,0:T(1,128)} %param.14) | copy-start | bytes 100
  29.8 28.6 %copy-start = (f32[3,128,1024]{2,1,0:T(8,128)S(1)}, f32[3,128,1024]{2,1,0:T(8,128)}, u32[]{:S(2)}) copy-start(f32[3,128,1024]{2,1,0:T(8,128)} %velocity.1) | copy-start | bytes 4718596
  36.5 17.8 %collective-permute-start.3 = (f32[3,128,256]{2,1,0:T(8,128)}, f32[3,128,256]{2,1,0:T(8,128)S(1)}, u32[]{:S(2)}, u32[]{:S(2)}) collective-permute-start(f32[3,128,256]{2,1,0:T(8,128)} %get-tuple-element.61), channel_id=1, source_target_pairs={{0,1},{1,0},{2,3},{3,2},{4,5},{5,4},{6,7},{7,6},{8,9},{9,8},{10,11... | collective-permute-start | bytes 1179656 | tf_op jit(solution)/shard_map/ppermute | solution.py:316
  36.6 17.7 %collective-permute-start.4 = (f32[3,128,256]{2,1,0:T(8,128)}, f32[3,128,256]{2,1,0:T(8,128)S(1)}, u32[]{:S(2)}, u32[]{:S(2)}) collective-permute-start(f32[3,128,256]{2,1,0:T(8,128)} %get-tuple-element.62), channel_id=1, source_target_pairs={{0,2},{1,3},{2,0},{3,1},{4,6},{5,7},{6,4},{7,5},{8,10},{9,11},{10,... | collective-permute-start | bytes 1179656 | tf_op jit(solution)/shard_map/ppermute | solution.py:316
  38.9 19.5 %collective-permute-start.5 = (f32[3,128,256]{2,1,0:T(8,128)}, f32[3,128,256]{2,1,0:T(8,128)S(1)}, u32[]{:S(2)}, u32[]{:S(2)}) collective-permute-start(f32[3,128,256]{2,1,0:T(8,128)} %get-tuple-element.63), channel_id=1, source_target_pairs={{0,3},{1,2},{2,1},{3,0},{4,7},{5,6},{6,5},{7,4},{8,11},{9,10},{10,... | collective-permute-start | bytes 1179656 | tf_op jit(solution)/shard_map/ppermute | solution.py:316
  40.1 1.0 copy-start.2
  43.6 9.9 %collective-permute-start.7 = (f32[64,128]{1,0:T(8,128)S(1)}, f32[64,128]{1,0:T(8,128)S(1)}, u32[]{:S(2)}, u32[]{:S(2)}) collective-permute-start(f32[64,128]{1,0:T(8,128)S(1)} %get-tuple-element.66.dgs), channel_id=1, source_target_pairs={{0,4},{4,8},{8,12},{12,16},{16,20},{20,24},{24,28},{28,32},{32,36}... | collective-permute-start | bytes 98312 | tf_op jit(solution)/shard_map/ppermute | solution.py:319
  45.2 8.4 %collective-permute-start.6 = (f32[64,128]{1,0:T(8,128)S(1)}, f32[64,128]{1,0:T(8,128)S(1)}, u32[]{:S(2)}, u32[]{:S(2)}) collective-permute-start(f32[64,128]{1,0:T(8,128)S(1)} %get-tuple-element.67.dgh), channel_id=1, source_target_pairs={{4,0},{8,4},{12,8},{16,12},{20,16},{24,20},{28,24},{32,28},{36,32}... | collective-permute-start | bytes 98312 | tf_op jit(solution)/shard_map/ppermute | solution.py:320
  61.2 11.2 %collective-permute-start.9 = (f32[64,384]{1,0:T(8,128)S(1)}, f32[64,384]{1,0:T(8,128)S(1)}, u32[]{:S(2)}, u32[]{:S(2)}) collective-permute-start(f32[64,384]{1,0:T(8,128)S(1)} %get-tuple-element.71.fs), channel_id=1, source_target_pairs={{0,4},{4,8},{8,12},{12,16},{16,20},{20,24},{24,28},{28,32},{32,36}... | collective-permute-start | bytes 294920 | tf_op jit(solution)/shard_map/ppermute | solution.py:319
  62.1 10.4 %collective-permute-start.8 = (f32[64,384]{1,0:T(8,128)S(1)}, f32[64,384]{1,0:T(8,128)S(1)}, u32[]{:S(2)}, u32[]{:S(2)}) collective-permute-start(f32[64,384]{1,0:T(8,128)S(1)} %get-tuple-element.72.fhalo), channel_id=1, source_target_pairs={{4,0},{8,4},{12,8},{16,12},{20,16},{24,20},{28,24},{32,28},{36,32}... | collective-permute-start | bytes 294920 | tf_op jit(solution)/shard_map/ppermute | solution.py:320
  72.7 8.9 %collective-permute-start.11 = (f32[64,384]{1,0:T(8,128)S(1)}, f32[64,384]{1,0:T(8,128)S(1)}, u32[]{:S(2)}, u32[]{:S(2)}) collective-permute-start(f32[64,384]{1,0:T(8,128)S(1)} %get-tuple-element.75.ps), channel_id=1, source_target_pairs={{0,4},{4,8},{8,12},{12,16},{16,20},{20,24},{24,28},{28,32},{32,36}... | collective-permute-start | bytes 294920 | tf_op jit(solution)/shard_map/ppermute | solution.py:319
  72.7 8.8 %collective-permute-start.10 = (f32[64,384]{1,0:T(8,128)S(1)}, f32[64,384]{1,0:T(8,128)S(1)}, u32[]{:S(2)}, u32[]{:S(2)}) collective-permute-start(f32[64,384]{1,0:T(8,128)S(1)} %get-tuple-element.76.ph), channel_id=1, source_target_pairs={{4,0},{8,4},{12,8},{16,12},{20,16},{24,20},{28,24},{32,28},{36,32}... | collective-permute-start | bytes 294920 | tf_op jit(solution)/shard_map/ppermute | solution.py:320
  81.8 8.9 %collective-permute-start.13 = (f32[64,384]{1,0:T(8,128)S(1)}, f32[64,384]{1,0:T(8,128)S(1)}, u32[]{:S(2)}, u32[]{:S(2)}) collective-permute-start(f32[64,384]{1,0:T(8,128)S(1)} %get-tuple-element.83.ps), channel_id=1, source_target_pairs={{0,4},{4,8},{8,12},{12,16},{16,20},{20,24},{24,28},{28,32},{32,36}... | collective-permute-start | bytes 294920 | tf_op jit(solution)/shard_map/ppermute | solution.py:319
  81.9 8.8 %collective-permute-start.12 = (f32[64,384]{1,0:T(8,128)S(1)}, f32[64,384]{1,0:T(8,128)S(1)}, u32[]{:S(2)}, u32[]{:S(2)}) collective-permute-start(f32[64,384]{1,0:T(8,128)S(1)} %get-tuple-element.84.ph), channel_id=1, source_target_pairs={{4,0},{8,4},{12,8},{16,12},{20,16},{24,20},{28,24},{32,28},{36,32}... | collective-permute-start | bytes 294920 | tf_op jit(solution)/shard_map/ppermute | solution.py:320
  91.0 9.0 %collective-permute-start.15 = (f32[64,384]{1,0:T(8,128)S(1)}, f32[64,384]{1,0:T(8,128)S(1)}, u32[]{:S(2)}, u32[]{:S(2)}) collective-permute-start(f32[64,384]{1,0:T(8,128)S(1)} %get-tuple-element.88.ps), channel_id=1, source_target_pairs={{0,4},{4,8},{8,12},{12,16},{16,20},{20,24},{24,28},{28,32},{32,36}... | collective-permute-start | bytes 294920 | tf_op jit(solution)/shard_map/ppermute | solution.py:319
  91.1 8.9 %collective-permute-start.14 = (f32[64,384]{1,0:T(8,128)S(1)}, f32[64,384]{1,0:T(8,128)S(1)}, u32[]{:S(2)}, u32[]{:S(2)}) collective-permute-start(f32[64,384]{1,0:T(8,128)S(1)} %get-tuple-element.89.ph), channel_id=1, source_target_pairs={{4,0},{8,4},{12,8},{16,12},{20,16},{24,20},{28,24},{32,28},{36,32}... | collective-permute-start | bytes 294920 | tf_op jit(solution)/shard_map/ppermute | solution.py:320
  100.3 9.0 %collective-permute-start.17 = (f32[64,384]{1,0:T(8,128)S(1)}, f32[64,384]{1,0:T(8,128)S(1)}, u32[]{:S(2)}, u32[]{:S(2)}) collective-permute-start(f32[64,384]{1,0:T(8,128)S(1)} %get-tuple-element.93.ps), channel_id=1, source_target_pairs={{0,4},{4,8},{8,12},{12,16},{16,20},{20,24},{24,28},{28,32},{32,36}... | collective-permute-start | bytes 294920 | tf_op jit(solution)/shard_map/ppermute | solution.py:319
  100.4 8.9 %collective-permute-start.16 = (f32[64,384]{1,0:T(8,128)S(1)}, f32[64,384]{1,0:T(8,128)S(1)}, u32[]{:S(2)}, u32[]{:S(2)}) collective-permute-start(f32[64,384]{1,0:T(8,128)S(1)} %get-tuple-element.94.ph), channel_id=1, source_target_pairs={{4,0},{8,4},{12,8},{16,12},{20,16},{24,20},{28,24},{32,28},{36,32}... | collective-permute-start | bytes 294920 | tf_op jit(solution)/shard_map/ppermute | solution.py:320
  109.5 9.2 %collective-permute-start.19 = (f32[64,384]{1,0:T(8,128)S(1)}, f32[64,384]{1,0:T(8,128)S(1)}, u32[]{:S(2)}, u32[]{:S(2)}) collective-permute-start(f32[64,384]{1,0:T(8,128)S(1)} %get-tuple-element.98.ps), channel_id=1, source_target_pairs={{0,4},{4,8},{8,12},{12,16},{16,20},{20,24},{24,28},{28,32},{32,36}... | collective-permute-start | bytes 294920 | tf_op jit(solution)/shard_map/ppermute | solution.py:319
  109.6 9.1 %collective-permute-start.18 = (f32[64,384]{1,0:T(8,128)S(1)}, f32[64,384]{1,0:T(8,128)S(1)}, u32[]{:S(2)}, u32[]{:S(2)}) collective-permute-start(f32[64,384]{1,0:T(8,128)S(1)} %get-tuple-element.99.ph), channel_id=1, source_target_pairs={{4,0},{8,4},{12,8},{16,12},{20,16},{24,20},{28,24},{32,28},{36,32}... | collective-permute-start | bytes 294920 | tf_op jit(solution)/shard_map/ppermute | solution.py:320
  119.0 9.0 %collective-permute-start.21 = (f32[64,384]{1,0:T(8,128)S(1)}, f32[64,384]{1,0:T(8,128)S(1)}, u32[]{:S(2)}, u32[]{:S(2)}) collective-permute-start(f32[64,384]{1,0:T(8,128)S(1)} %get-tuple-element.103.ps), channel_id=1, source_target_pairs={{0,4},{4,8},{8,12},{12,16},{16,20},{20,24},{24,28},{28,32},{32,36}... | collective-permute-start | bytes 294920 | tf_op jit(solution)/shard_map/ppermute | solution.py:319
  119.1 8.9 %collective-permute-start.20 = (f32[64,384]{1,0:T(8,128)S(1)}, f32[64,384]{1,0:T(8,128)S(1)}, u32[]{:S(2)}, u32[]{:S(2)}) collective-permute-start(f32[64,384]{1,0:T(8,128)S(1)} %get-tuple-element.104.ph), channel_id=1, source_target_pairs={{4,0},{8,4},{12,8},{16,12},{20,16},{24,20},{28,24},{32,28},{36,32}... | collective-permute-start | bytes 294920 | tf_op jit(solution)/shard_map/ppermute | solution.py:320
  128.3 9.3 %collective-permute-start.23 = (f32[64,384]{1,0:T(8,128)S(1)}, f32[64,384]{1,0:T(8,128)S(1)}, u32[]{:S(2)}, u32[]{:S(2)}) collective-permute-start(f32[64,384]{1,0:T(8,128)S(1)} %get-tuple-element.108.ps), channel_id=1, source_target_pairs={{0,4},{4,8},{8,12},{12,16},{16,20},{20,24},{24,28},{28,32},{32,36}... | collective-permute-start | bytes 294920 | tf_op jit(solution)/shard_map/ppermute | solution.py:319
  128.3 9.2 %collective-permute-start.22 = (f32[64,384]{1,0:T(8,128)S(1)}, f32[64,384]{1,0:T(8,128)S(1)}, u32[]{:S(2)}, u32[]{:S(2)}) collective-permute-start(f32[64,384]{1,0:T(8,128)S(1)} %get-tuple-element.109.ph), channel_id=1, source_target_pairs={{4,0},{8,4},{12,8},{16,12},{20,16},{24,20},{28,24},{32,28},{36,32}... | collective-permute-start | bytes 294920 | tf_op jit(solution)/shard_map/ppermute | solution.py:320
